TPU v7x, 512 devices: a whole 4x8x8 slice. The times are simulated.
512 devices in a mesh: member: 4 (over x), shard: 128 (over y, z, core).
Axes of the slice: x: 4, y: 8, z: 8, core: 2. Of those that a mesh axis runs over, the one named last changes fastest.
Arguments:
- teacher_hidden: bfloat16 [4, 2048, 4096], P('member', 'shard'), may hold values from -80 to 80
- teacher_gain: float32 [4, 4096], P('member'), may hold values from 0.1 to 1.9
- teacher_head: bfloat16 [4, 4096, 65536], P('member', None, 'shard'), may hold values from -0.5 to 0.5
- student_hidden: bfloat16 [2048, 2048], P('shard', 'member'), may hold values from -8 to 8
- student_head: bfloat16 [2048, 65536], P('member', 'shard'), may hold values from -0.6 to 0.6
- positions: int32 [128, 4], P('shard'), may hold values from 0 to 15, as said below
- counts: int32 [128], replicated, may hold values from 1 to 4, 256 in all
- targets: int32 [512], replicated, may hold values from 0 to 65535
Outputs:
- mean_loss: float32 [], replicated
- hidden_grad: bfloat16 [2048, 2048], P('shard', 'member')
Inputs may be any that keep to these rules, and one draw needn't show every extreme that they name: Each owner's positions are distinct. The counts sum to exactly 256.
All inputs are finite; a program needn't handle non-finite values.
Results may differ from a plain program's by a relative error of at most 0.0039.
Values may be sent and summed in bfloat16 or wider, within the bound.
No kernel may reach another device: no remote copies, remote signals or barrier semaphores. Data moves between devices by JAX's collectives and lax.ppermute only.
A program may use at most 64 MiB of HBM per device.

v0:
```python
import jax
import jax.numpy as jnp
from jax import lax
from jax.sharding import PartitionSpec as P

LOSS_SCALE = 16.0
BLEND = 0.5
EPS = 1e-05


def vocab_stats(logits):
    local_top = jnp.max(logits, axis=1)
    highest = lax.pmax(local_top, "shard")
    totals = lax.psum(jnp.sum(jnp.exp(logits - highest[:, None]), axis=1), "shard")
    return (highest, totals)


def on_device(
    teacher_hidden,
    teacher_gain,
    teacher_head,
    student_hidden,
    student_head,
    positions,
    counts,
    targets,
):
    owners = lax.axis_size("shard")
    members = lax.axis_size("member")
    owner_rank = lax.axis_index("shard")
    slot_ids = positions[0]
    per_owner = slot_ids.shape[0]
    vocab_part = student_head.shape[1]
    window_rows = student_hidden.shape[0]
    widened = jnp.take(teacher_hidden[0], slot_ids, axis=0).astype(jnp.float32)
    inverse_rms = lax.rsqrt(jnp.mean(widened * widened, axis=1, keepdims=True) + EPS)
    normed = (widened * inverse_rms * teacher_gain[0][None, :]).astype(jnp.bfloat16)
    student_picked = jnp.take(student_hidden, slot_ids, axis=0)
    teacher_rows, student_rows = (
        lax.all_gather(normed, "shard", axis=0, tiled=True),
        lax.all_gather(student_picked, "shard", axis=0, tiled=True),
    )
    padded_rows = per_owner * owners
    padded_ids = jnp.arange(padded_rows, dtype=jnp.int32)
    padded_slot = padded_ids % per_owner
    owner_counts = jnp.repeat(counts, per_owner, total_repeat_length=padded_rows)
    padded_weight = (padded_slot < owner_counts).astype(jnp.float32)
    teacher_logits = jnp.dot(teacher_rows, teacher_head[0], preferred_element_type=jnp.float32)
    highest, totals = vocab_stats(teacher_logits)
    teacher_probs = jnp.exp(teacher_logits - highest[:, None]) / totals[:, None]
    partial_logits = jnp.dot(student_rows, student_head, preferred_element_type=jnp.float32)
    student_logits, prob_sums = lax.psum((partial_logits, teacher_probs), "member")
    mean_probs = prob_sums / members
    highest, totals = vocab_stats(student_logits)
    log_total = highest + jnp.log(totals)
    vocab_ids = owner_rank * vocab_part + jnp.arange(vocab_part, dtype=jnp.int32)
    onehot = (vocab_ids[None, :] == targets[:, None]).astype(jnp.float32)
    mixture = BLEND * onehot + (1.0 - BLEND) * mean_probs
    cross_part = jnp.sum(padded_weight * jnp.sum(mixture * student_logits, axis=1))
    lse_part = jnp.where(owner_rank == 0, jnp.sum(padded_weight * log_total), 0.0)
    loss_term = lse_part - cross_part
    slope_rows = (
        LOSS_SCALE
        * padded_weight[:, None]
        * (jnp.exp(student_logits - log_total[:, None]) - mixture)
    ).astype(jnp.bfloat16)
    loss_total = lax.psum(loss_term, "shard")
    mean_loss = loss_total / jnp.sum(counts).astype(jnp.float32)
    chosen = lax.slice_in_dim(slope_rows, 0, per_owner * lax.axis_size("shard"), axis=0)
    slot_grad = lax.psum_scatter(
        lax.dot_general(
            chosen, student_head, (((1,), (1,)), ((), ())), preferred_element_type=jnp.float32
        ),
        "shard",
        scatter_dimension=0,
        tiled=True,
    )
    placed = (jnp.arange(window_rows, dtype=jnp.int32)[:, None] == slot_ids[None, :]).astype(
        jnp.float32
    )
    hidden_grad = jnp.sum(placed[:, :, None] * slot_grad[None, :, :], axis=1).astype(jnp.bfloat16)
    return (mean_loss, hidden_grad)


def solution(mesh):
    placed = (
        P("member", "shard", None),
        P("member", None),
        P("member", None, "shard"),
        P("shard", "member"),
        P("member", "shard"),
        P("shard", None),
        P(),
        P(),
    )
    return jax.shard_map(
        on_device,
        mesh=mesh,
        in_specs=placed,
        out_specs=(P(), P("shard", "member")),
        check_vma=False,
    )
```

profile of v0, /device:TPU:1, one launch (start us, length us, event | category | flops | bytes accessed | tf_op | source)
XLA Modules:
  0.0 1239.3 jit_solution(6478698741609276838)
XLA Ops:
  8.0 0.0 copy-start
  8.0 0.0 all-reduce.6.cloned.1.call-start
  8.1 0.7 fusion.23
  8.8 0.7 compare_and_fusion
  9.5 1.3 gather_fusion.1
  10.7 0.1 select_bitcast_fusion
  10.8 58.9 %all-gather = bf16[128,4,512]{2,1,0:T(4,128)(2,1)S(1)} all-gather(bf16[1,4,512]{2,1,0:T(4,128)(2,1)S(1)} %select_bitcast_fusion), channel_id=1, replica_groups=mesh['member'=4,'shard'=128] {'shard'}, dimensions={0}, use_global_device_ids=true | all-gather | bytes 528384 | tf_op jit(solution)/shard_map/all_gather | solution.py:41
  69.8 0.1 reshape.234
  69.9 1.4 fusion.29
  71.3 0.0 all-reduce.6.cloned.1.call-update
  71.3 0.0 all-gather.4.cloned.1.call-start
  71.4 0.0 copy-done.3
  71.4 0.6 gather_fusion.2
  72.0 0.2 fusion.12
  72.2 0.7 fusion.15
  72.9 0.0 all-gather.4.cloned.1.call-update
  72.9 0.0 all-reduce.8.cloned.1.call-start
  73.0 48.6 %all-reduce.6.cloned.1.call-done = f32[512,512]{1,0:T(8,128)} async-done(((f32[512,512]{1,0:T(8,128)}), f32[512,512]{1,0:T(8,128)}) %all-reduce.6.cloned.1.call-update) | async-done | bytes 1048592 | tf_op jit(solution)/shard_map/psum | solution.py:52
  121.6 1.4 reduce_max.18
  123.0 32.7 %all-gather.4.cloned.1.call-done = bf16[128,4,4096]{2,1,0:T(4,128)(2,1)} async-done(((bf16[1,4,4096]{2,1,0:T(4,128)(2,1)}), bf16[128,4,4096]{2,1,0:T(4,128)(2,1)}) %all-gather.4.cloned.1.call-update) | async-done | bytes 4194320 | tf_op jit(solution)/shard_map/all_gather | solution.py:40
  155.6 6.9 reshape.236
  162.6 6.8 fusion.28
  169.4 0.0 copy-start.5
  169.4 1.6 copy.13
  171.1 246.4 %all-reduce.1 = (f32[512]{0:T(512)S(1)}, f32[512]{0:T(512)S(1)}) all-reduce(f32[512]{0:T(512)S(1)} %reduce_max.18, f32[512]{0:T(512)S(1)} %get-tuple-element.25), channel_id=1, replica_groups=mesh['member'=4,'shard'=128] {'shard'}, use_global_device_ids=true, to_apply=%region_2.3 | all-reduce | flops 1024 | bytes 8192 | tf_op jit(solution)/shard_map/pmax | solution.py:13
  417.5 0.3 fusion.3
  417.8 249.4 %psum.37 = f32[512]{0:T(512)S(1)} all-reduce(f32[512]{0:T(512)S(1)} %fusion.3), channel_id=1, replica_groups=mesh['member'=4,'shard'=128] {'shard'}, use_global_device_ids=true, to_apply=%region_10.11 | all-reduce | flops 512 | bytes 4096 | tf_op jit(solution)/shard_map/psum | solution.py:14
  667.2 1.3 fusion.2
  668.4 0.0 all-reduce.8.cloned.1.call-update
  668.5 0.0 all-reduce.10.cloned.1.call-start
  668.5 0.1 add_add_fusion.1
  668.6 0.0 copy-start.7
  668.7 3.3 gather_fusion
  672.0 46.3 %all-reduce.8.cloned.1.call-done = f32[512,512]{1,0:T(8,128)} async-done(((f32[512,512]{1,0:T(8,128)}), f32[512,512]{1,0:T(8,128)}) %all-reduce.8.cloned.1.call-update) | async-done | bytes 1048592 | tf_op jit(solution)/shard_map/psum | solution.py:52
  718.4 0.0 copy-done.2
  718.4 1.8 multiply_reduce_fusion
  720.1 249.5 %psum.36 = f32[512]{0:T(512)S(1)} all-reduce(f32[512]{0:T(512)S(1)} %get-tuple-element.15), channel_id=1, replica_groups=mesh['member'=4,'shard'=128] {'shard'}, use_global_device_ids=true, to_apply=%region_4.5 | all-reduce | flops 512 | bytes 4096 | tf_op jit(solution)/shard_map/psum | solution.py:14
  969.6 0.6 broadcast_select_fusion.1
  970.2 0.6 select_reduce_fusion.1
  970.9 2.8 fusion.4
  973.7 0.0 all-reduce.10.cloned.1.call-update
  973.7 0.6 reduce_sum.78
  975.0 1.3 dynamic-slice.6
  976.3 0.1 fusion.22
  978.3 250.4 %psum.39 = f32[]{:T(128)} all-reduce(f32[]{:T(128)S(6)} %sub.51), channel_id=1, replica_groups=mesh['member'=4,'shard'=128] {'shard'}, use_global_device_ids=true, to_apply=%region_14.15 | all-reduce | flops 1 | bytes 8 | tf_op jit(solution)/shard_map/psum | solution.py:67
  1229.3 0.0 all-reduce.10.cloned.1.call-done
  1229.4 0.7 constant_dynamic-slice_fusion
  1230.1 0.7 multiply_reduce_fusion.1
  (17 shorter events, 0.1 us)
Async XLA Ops:
  8.0 61.9 %copy-start = (bf16[512,512]{1,0:T(8,128)(2,1)S(1)}, bf16[512,512]{1,0:T(8,128)(2,1)}, u32[]{:S(2)}) copy-start(bf16[512,512]{1,0:T(8,128)(2,1)} %param.14) | copy-start | bytes 1572868
  8.0 63.4 %copy-start.3 = (bf16[1,16,4096]{2,1,0:T(8,128)(2,1)S(1)}, bf16[1,16,4096]{2,1,0:T(8,128)(2,1)}, u32[]{:S(2)}) copy-start(bf16[1,16,4096]{2,1,0:T(8,128)(2,1)} %param.10) | copy-start | bytes 393220
  8.0 64.2 %copy-start.4 = (f32[1,4096]{1,0:T(1,128)S(1)}, f32[1,4096]{1,0:T(1,128)}, u32[]{:S(2)}) copy-start(f32[1,4096]{1,0:T(1,128)} %param.11) | copy-start | bytes 49156
  8.0 113.6 %all-reduce.6.cloned.1.call-start = ((), (), s32[]{:S(2)}) async-start(), calls=%async_computation | async-start | bytes 2097152 | tf_op jit(solution)/shard_map/psum | solution.py:52
  71.3 84.3 %all-gather.4.cloned.1.call-start = ((), (), s32[]{:S(2)}) async-start(), calls=%async_computation.2 | async-start | bytes 4227072 | tf_op jit(solution)/shard_map/all_gather | solution.py:40
  72.9 645.4 %all-reduce.8.cloned.1.call-start = ((), (), s32[]{:S(2)}) async-start(), calls=%async_computation.1 | async-start | bytes 2097152 | tf_op jit(solution)/shard_map/psum | solution.py:52
  169.4 499.2 %copy-start.6 = (s32[4,128]{1,0:T(4,128)S(1)}, s32[4,128]{1,0:T(4,128)}, u32[]{:S(2)}) copy-start(s32[4,128]{1,0:T(4,128)} %constant.159.clone.1) | copy-start | bytes 6148
  169.4 499.3 %copy-start.1 = (s32[128]{0:T(128)S(1)}, s32[128]{0:T(128)}, u32[]{:S(2)}) copy-start(s32[128]{0:T(128)} %param.16) | copy-start | bytes 1540
  169.4 549.0 %copy-start.2 = (f32[512,512]{1,0:T(8,128)S(1)}, f32[512,512]{1,0:T(8,128)}, u32[]{:S(2)}) copy-start(f32[512,512]{1,0:T(8,128)} %all-reduce.6.cloned.1.call-done) | copy-start | bytes 3145732
  169.4 549.0 %copy-start.5 = (s32[512]{0:T(512)S(1)}, s32[512]{0:T(512)}, u32[]{:S(2)}) copy-start(s32[512]{0:T(512)} %param.17) | copy-start | bytes 6148
  668.5 560.9 %all-reduce.10.cloned.1.call-start = ((), (), s32[]{:S(2)}) async-start(), calls=%async_computation.3 | async-start | bytes 2097152
  668.6 307.6 %copy-start.7 = (s32[1,4]{1,0:T(1,128)S(1)}, s32[1,4]{1,0:T(1,128)}, u32[]{:S(2)}) copy-start(s32[1,4]{1,0:T(1,128)} %param.15) | copy-start | bytes 52
Sparse Core Ops, SparseCore 0:
  71.5 50.0 all-reduce.5
  668.6 49.7 all-reduce.7
Sparse Core Ops, SparseCore 1:
  75.4 80.2 all-gather.3
  973.8 190.7 all-reduce.9
where the time goes:
time: 1240 us
  blocking collectives  1050 us (85%)
  waiting for transfers between devices  128 us (10%)
  between operations  20 us (2%)
  local copies, waits for them, and re-layouts  15.9 us (1%)
    psum x2, blocking collectives, vocab_stats(): lax.psum(jnp.sum(jnp.exp(logits - highest[:, None]), axis=1), 'shard')  499 us
    psum x1, blocking collectives, on_device(): loss_total = lax.psum(loss_term, 'shard')  250 us
    pmax x1, blocking collectives, vocab_stats(): highest = lax.pmax(local_top, 'shard')  246 us
    psum x2, waiting for transfers between devices, on_device(): lax.psum((partial_logits, teacher_probs), 'member')  94.9 us
    all_gather x1, blocking collectives, on_device(): lax.all_gather(student_picked, 'shard', axis=0, tiled=True)  58.9 us
    all_gather x1, waiting for transfers between devices, on_device(): lax.all_gather(normed, 'shard', axis=0, tiled=True)  32.7 us
  transfers between devices with their start and end apart: 4, of which 3 were waited for; matrix products, arithmetic and copies ran while one was open for 1% of the time, Pallas kernels for 0%

commit v1 on v0

--- a/solution.py
+++ b/solution.py
@@ -11,7 +11,9 @@
 def vocab_stats(logits):
     local_top = jnp.max(logits, axis=1)
     highest = lax.pmax(local_top, "shard")
-    totals = lax.psum(jnp.sum(jnp.exp(logits - highest[:, None]), axis=1), "shard")
+    totals = jnp.sum(
+        lax.all_gather(jnp.sum(jnp.exp(logits - highest[:, None]), axis=1), "shard"), axis=0
+    )
     return (highest, totals)
 
 

time: 1240 us -> 845 us (0.68)
  blocking collectives: 1050 us -> 656 us
    psum x2 -> x0, blocking collectives: 499 us -> none  [vocab_stats(): lax.psum(jnp.sum(jnp.exp(logits - highest[:, None]), axis=1), 'shard')]
    all_gather x0 -> x2, blocking collectives: none -> 103 us  [vocab_stats(): lax.all_gather(jnp.sum(jnp.exp(logits - highest[:, None]), axis=1), 'shard')]
where the time goes in v1:
time: 845 us; the launch traced here: 843 us
  blocking collectives  656 us (78%)
  waiting for transfers between devices  130 us (15%)
  between operations  20 us (2%)
  local copies, waits for them, and re-layouts  15.9 us (2%)
  matrix products  11.1 us (1%)
  other arithmetic  10.2 us (1%)
    psum x1, blocking collectives, on_device(): loss_total = lax.psum(loss_term, 'shard')  247 us
    pmax x1, blocking collectives, vocab_stats(): highest = lax.pmax(local_top, 'shard')  246 us
    all_gather x2, blocking collectives, vocab_stats(): lax.all_gather(jnp.sum(jnp.exp(logits - highest[:, None]), axis=1), 'shard')  103 us
    psum x2, waiting for transfers between devices, on_device(): lax.psum((partial_logits, teacher_probs), 'member')  97 us
    all_gather x1, blocking collectives, on_device(): lax.all_gather(student_picked, 'shard', axis=0, tiled=True)  58.9 us
    all_gather x1, waiting for transfers between devices, on_device(): lax.all_gather(normed, 'shard', axis=0, tiled=True)  32.7 us
  transfers between devices with their start and end apart: 4, of which 3 were waited for; matrix products, arithmetic and copies ran while one was open for 1% of the time, Pallas kernels for 0%

profile of v1, /device:TPU:1, one launch (start us, length us, event | category | flops | bytes accessed | tf_op | source)
XLA Modules:
  0.0 842.7 jit_solution(2970128637504450885)
XLA Ops:
  8.0 0.0 copy-start
  8.0 0.0 all-reduce.6.cloned.1.call-start
  8.1 0.7 fusion.23
  8.8 0.7 compare_and_fusion
  9.5 1.3 gather_fusion.1
  10.7 0.1 select_bitcast_fusion
  10.8 58.9 %all-gather.2 = bf16[128,4,512]{2,1,0:T(4,128)(2,1)S(1)} all-gather(bf16[1,4,512]{2,1,0:T(4,128)(2,1)S(1)} %select_bitcast_fusion), channel_id=1, replica_groups=mesh['member'=4,'shard'=128] {'shard'}, dimensions={0}, use_global_device_ids=true | all-gather | bytes 528384 | tf_op jit(solution)/shard_map/all_gather | solution.py:43
  69.8 0.1 reshape.236
  69.9 1.4 fusion.29
  71.3 0.0 all-reduce.6.cloned.1.call-update
  71.3 0.0 all-gather.8.cloned.1.call-start
  71.4 0.6 gather_fusion.2
  72.0 0.2 fusion.12
  72.2 0.7 fusion.15
  72.9 0.0 all-gather.8.cloned.1.call-update
  72.9 0.0 all-reduce.8.cloned.1.call-start
  73.0 48.6 %all-reduce.6.cloned.1.call-done = f32[512,512]{1,0:T(8,128)} async-done(((f32[512,512]{1,0:T(8,128)}), f32[512,512]{1,0:T(8,128)}) %all-reduce.6.cloned.1.call-update) | async-done | bytes 1048592 | tf_op jit(solution)/shard_map/psum | solution.py:54
  121.6 1.4 reduce_max.18
  123.0 32.7 %all-gather.8.cloned.1.call-done = bf16[128,4,4096]{2,1,0:T(4,128)(2,1)} async-done(((bf16[1,4,4096]{2,1,0:T(4,128)(2,1)}), bf16[128,4,4096]{2,1,0:T(4,128)(2,1)}) %all-gather.8.cloned.1.call-update) | async-done | bytes 4194320 | tf_op jit(solution)/shard_map/all_gather | solution.py:42
  155.6 6.9 reshape.240
  162.6 6.8 fusion.28
  169.4 0.0 copy-start.5
  169.4 1.6 copy.13
  171.1 246.4 %all-reduce.1 = (f32[512]{0:T(512)S(1)}, f32[512]{0:T(512)S(1)}) all-reduce(f32[512]{0:T(512)S(1)} %reduce_max.18, f32[512]{0:T(512)S(1)} %get-tuple-element.25), channel_id=1, replica_groups=mesh['member'=4,'shard'=128] {'shard'}, use_global_device_ids=true, to_apply=%region_2.3 | all-reduce | flops 1024 | bytes 8192 | tf_op jit(solution)/shard_map/pmax | solution.py:13
  417.5 0.3 fusion.3
  417.8 49.8 %all-gather.5 = f32[128,1,512]{2,1,0:T(1,128)S(1)} all-gather(f32[1,1,512]{2,1,0:T(1,128)S(1)} %bitcast.44), channel_id=3, replica_groups=mesh['member'=4,'shard'=128] {'shard'}, dimensions={0}, use_global_device_ids=true | all-gather | bytes 264192 | tf_op jit(solution)/shard_map/all_gather | solution.py:15
  467.6 0.2 reduce_sum.95
  467.8 1.3 fusion.2
  469.0 0.0 all-reduce.8.cloned.1.call-update
  469.0 0.0 all-reduce.10.cloned.1.call-start
  469.1 0.1 add_add_fusion.1
  469.2 3.3 gather_fusion
  472.6 0.0 copy-start.7
  472.6 48.4 %all-reduce.8.cloned.1.call-done = f32[512,512]{1,0:T(8,128)} async-done(((f32[512,512]{1,0:T(8,128)}), f32[512,512]{1,0:T(8,128)}) %all-reduce.8.cloned.1.call-update) | async-done | bytes 1048592 | tf_op jit(solution)/shard_map/psum | solution.py:54
  521.0 1.8 multiply_reduce_fusion
  522.8 53.5 %all-gather.3 = f32[128,1,512]{2,1,0:T(1,128)S(1)} all-gather(f32[1,1,512]{2,1,0:T(1,128)S(1)} %bitcast.43), channel_id=2, replica_groups=mesh['member'=4,'shard'=128] {'shard'}, dimensions={0}, use_global_device_ids=true | all-gather | bytes 264192 | tf_op jit(solution)/shard_map/all_gather | solution.py:15
  576.3 0.2 reduce_sum.91
  576.5 0.6 broadcast_select_fusion.1
  577.1 0.6 select_reduce_fusion.1
  577.8 2.8 fusion.4
  580.6 0.0 all-reduce.10.cloned.1.call-update
  580.6 0.6 reduce_sum.98
  581.9 1.3 dynamic-slice.6
  583.2 0.1 fusion.22
  585.2 246.9 %psum.23 = f32[]{:T(128)} all-reduce(f32[]{:T(128)S(6)} %sub.51), channel_id=1, replica_groups=mesh['member'=4,'shard'=128] {'shard'}, use_global_device_ids=true, to_apply=%region_14.15 | all-reduce | flops 1 | bytes 8 | tf_op jit(solution)/shard_map/psum | solution.py:69
  832.7 0.0 all-reduce.10.cloned.1.call-done
  832.8 0.7 constant_dynamic-slice_fusion
  833.5 0.7 multiply_reduce_fusion.1
  (19 shorter events, 0.1 us)
Async XLA Ops:
  8.0 61.9 %copy-start = (bf16[512,512]{1,0:T(8,128)(2,1)S(1)}, bf16[512,512]{1,0:T(8,128)(2,1)}, u32[]{:S(2)}) copy-start(bf16[512,512]{1,0:T(8,128)(2,1)} %param.14) | copy-start | bytes 1572868
  8.0 63.4 %copy-start.3 = (bf16[1,16,4096]{2,1,0:T(8,128)(2,1)S(1)}, bf16[1,16,4096]{2,1,0:T(8,128)(2,1)}, u32[]{:S(2)}) copy-start(bf16[1,16,4096]{2,1,0:T(8,128)(2,1)} %param.10) | copy-start | bytes 393220
  8.0 64.2 %copy-start.4 = (f32[1,4096]{1,0:T(1,128)S(1)}, f32[1,4096]{1,0:T(1,128)}, u32[]{:S(2)}) copy-start(f32[1,4096]{1,0:T(1,128)} %param.11) | copy-start | bytes 49156
  8.0 113.6 %all-reduce.6.cloned.1.call-start = ((), (), s32[]{:S(2)}) async-start(), calls=%async_computation | async-start | bytes 2097152 | tf_op jit(solution)/shard_map/psum | solution.py:54
  71.3 84.3 %all-gather.8.cloned.1.call-start = ((), (), s32[]{:S(2)}) async-start(), calls=%async_computation.2 | async-start | bytes 4227072 | tf_op jit(solution)/shard_map/all_gather | solution.py:42
  72.9 448.1 %all-reduce.8.cloned.1.call-start = ((), (), s32[]{:S(2)}) async-start(), calls=%async_computation.1 | async-start | bytes 2097152 | tf_op jit(solution)/shard_map/psum | solution.py:54
  169.4 299.7 %copy-start.6 = (s32[4,128]{1,0:T(4,128)S(1)}, s32[4,128]{1,0:T(4,128)}, u32[]{:S(2)}) copy-start(s32[4,128]{1,0:T(4,128)} %constant.159.clone.1) | copy-start | bytes 6148
  169.4 299.8 %copy-start.1 = (s32[128]{0:T(128)S(1)}, s32[128]{0:T(128)}, u32[]{:S(2)}) copy-start(s32[128]{0:T(128)} %param.16) | copy-start | bytes 1540
  169.4 351.7 %copy-start.2 = (f32[512,512]{1,0:T(8,128)S(1)}, f32[512,512]{1,0:T(8,128)}, u32[]{:S(2)}) copy-start(f32[512,512]{1,0:T(8,128)} %all-reduce.6.cloned.1.call-done) | copy-start | bytes 3145732
  169.4 351.7 %copy-start.5 = (s32[512]{0:T(512)S(1)}, s32[512]{0:T(512)}, u32[]{:S(2)}) copy-start(s32[512]{0:T(512)} %param.17) | copy-start | bytes 6148
  469.0 363.7 %all-reduce.10.cloned.1.call-start = ((), (), s32[]{:S(2)}) async-start(), calls=%async_computation.3 | async-start | bytes 2097152
  472.6 110.6 %copy-start.7 = (s32[1,4]{1,0:T(1,128)S(1)}, s32[1,4]{1,0:T(1,128)}, u32[]{:S(2)}) copy-start(s32[1,4]{1,0:T(1,128)} %param.15) | copy-start | bytes 52
Sparse Core Ops, SparseCore 0:
  71.5 50.0 all-reduce.5
  469.2 51.8 all-reduce.7
Sparse Core Ops, SparseCore 1:
  75.4 80.2 all-gather.7
  580.7 191.2 all-reduce.9
